TPU v7x, 512 devices: a whole 4x8x8 slice. The times are simulated.
512 devices in a mesh: rows: 128 (over z, y, core), modes: 4 (over x).
Axes of the slice: x: 4, y: 8, z: 8, core: 2. Of those that a mesh axis runs over, the one named last changes fastest.
Arguments:
- modes_basis: float32 [256, 786432], P('modes', 'rows'), may hold values from -1 to 1
- snapshots: float32 [256, 786432], P('modes', 'rows'), may hold values from -40 to 40
Outputs:
- coefficients: float32 [256, 256], P('modes')
- residual: float32 [256, 786432], P('modes', 'rows')
- gram: float32 [256, 256], P('modes')
- residual_norm: float32 [256], P('modes')
All inputs are finite; a program needn't handle non-finite values.
Results may differ from a plain program's by a relative error of at most 0.00027.
Values sent between devices are 32-bit elements; how exact they have to be, the bound alone decides.
A program may use at most 64 MiB of HBM per device.

v0:
```python
import jax
import jax.numpy as jnp
from jax import lax
from jax.sharding import PartitionSpec as P


def product(left, right):
    return jnp.dot(left, right, preferred_element_type=jnp.float32, precision=lax.Precision.HIGHEST)


def per_device(modes_basis, snapshots):
    panel = lax.all_gather(modes_basis, "modes", axis=0, tiled=True)
    partial_value = product(snapshots, panel.T)
    coefficients = lax.psum(partial_value, "rows")
    residual = snapshots - product(coefficients, panel)
    total_rows = residual.shape[1] * lax.axis_size("rows")
    partial_gram = product(residual, lax.all_gather(residual, "modes", axis=0, tiled=True).T)
    gram = lax.psum(partial_gram, "rows") / total_rows
    squares = lax.psum(jnp.sum(residual * residual, axis=1), "rows")
    residual_norm = jnp.sqrt(squares / total_rows)
    return (coefficients, residual, gram, residual_norm)


def solution(mesh):
    in_specs = (P("modes", "rows"), P("modes", "rows"))
    out_specs = (P("modes", None), P("modes", "rows"), P("modes", None), P("modes"))
    return jax.shard_map(
        per_device, mesh=mesh, in_specs=in_specs, out_specs=out_specs, check_vma=False
    )
```

profile of v0, /device:TPU:1, one launch (start us, length us, event | category | flops | bytes accessed | tf_op | source)
XLA Modules:
  0.0 723.3 jit_solution(6048534676033143362)
XLA Ops:
  7.2 0.0 copy-start.1
  7.2 0.0 all-gather.3.cloned.1.call-start
  7.2 0.7 all-gather.3.cloned.1.call-update
  7.9 0.0 all-reduce.3.cloned.1.call-start
  8.0 78.7 %all-gather.3.cloned.1.call-done = f32[256,6144]{1,0:T(8,128)} async-done(((f32[64,6144]{1,0:T(8,128)}), f32[256,6144]{1,0:T(8,128)}) %all-gather.3.cloned.1.call-update) | async-done | bytes 6291472 | tf_op jit(solution)/shard_map/all_gather | solution.py:12
  86.6 0.0 copy-done.1
  86.6 8.5 %fusion = f32[64,256]{1,0:T(8,128)} fusion(f32[64,6144]{1,0:T(8,128)S(1)} %copy-done.1, f32[256,6144]{1,0:T(8,128)} %all-gather.3.cloned.1.call-done), kind=kOutput, calls=%fused_computation.4 | convolution fusion | flops 1207959552 | bytes 7929856 | tf_op jit(solution)/shard_map/dot_general | solution.py:8
  95.1 0.0 all-reduce.3.cloned.1.call-update
  95.2 0.0 all-gather.5.cloned.1.call-start
  95.2 181.5 %all-reduce.3.cloned.1.call-done = f32[64,256]{1,0:T(8,128)} async-done(((f32[64,256]{1,0:T(8,128)}), f32[64,256]{1,0:T(8,128)}) %all-reduce.3.cloned.1.call-update) | async-done | bytes 65552 | tf_op jit(solution)/shard_map/psum | solution.py:14
  276.7 7.9 %multiply_reduce_fusion = (f32[64]{0:T(128)S(1)}, f32[64,6144]{1,0:T(8,128)}) fusion(f32[64,6144]{1,0:T(8,128)S(1)} %copy-done.1, f32[64,256]{1,0:T(8,128)} %all-reduce.3.cloned.1.call-done, f32[256,6144]{1,0:T(8,128)} %all-gather.3.cloned.1.call-done), kind=kOutput, calls=%fused_computation.1 | convolution fusion | flops 1209139200 | bytes 9502976 | tf_op jit(solution)/shard_map/dot_general | solution.py:8
  284.6 0.0 copy-start
  284.6 0.0 all-gather.5.cloned.1.call-update
  284.7 0.0 all-reduce.5.cloned.1.call-start
  284.7 242.3 %psum.23 = f32[64]{0:T(128)S(1)} all-reduce(f32[64]{0:T(128)S(1)} %get-tuple-element.4), channel_id=1, replica_groups=mesh['rows'=128,'modes'=4] {'rows'}, use_global_device_ids=true, to_apply=%region_3.0 | all-reduce | flops 64 | bytes 512 | tf_op jit(solution)/shard_map/psum | solution.py:19
  527.0 0.0 copy-start.2
  527.0 0.0 all-gather.5.cloned.1.call-done
  527.0 0.0 copy-done
  527.0 8.5 %fusion.1 = f32[64,256]{1,0:T(8,128)} fusion(f32[64,6144]{1,0:T(8,128)S(1)} %copy-done, f32[256,6144]{1,0:T(8,128)} %all-gather.5.cloned.1.call-done), kind=kOutput, calls=%fused_computation.5 | convolution fusion | flops 1207959552 | bytes 7929856 | tf_op jit(solution)/shard_map/dot_general | solution.py:8
  535.5 0.0 all-reduce.5.cloned.1.call-update
  535.6 0.5 multiply_sqrt_fusion
  536.1 178.6 %all-reduce.5.cloned.1.call-done = f32[64,256]{1,0:T(8,128)} async-done(((f32[64,256]{1,0:T(8,128)}), f32[64,256]{1,0:T(8,128)}) %all-reduce.5.cloned.1.call-update) | async-done | bytes 65552 | tf_op jit(solution)/shard_map/psum | solution.py:18
  714.7 1.5 broadcast_multiply_fusion
  716.2 0.0 copy-done.2
  716.2 0.6 copy.8
Async XLA Ops:
  7.2 79.5 %copy-start.1 = (f32[64,6144]{1,0:T(8,128)S(1)}, f32[64,6144]{1,0:T(8,128)}, u32[]{:S(2)}) copy-start(f32[64,6144]{1,0:T(8,128)} %param.3) | copy-start | bytes 4718596
  7.2 79.4 %all-gather.3.cloned.1.call-start = ((), (), s32[]{:S(2)}) async-start(), calls=%async_computation | async-start | bytes 7864320 | tf_op jit(solution)/shard_map/all_gather | solution.py:12
  7.9 268.8 %all-reduce.3.cloned.1.call-start = ((), (), s32[]{:S(2)}) async-start(), calls=%async_computation.1 | async-start | bytes 131072 | tf_op jit(solution)/shard_map/psum | solution.py:14
  95.2 431.9 %all-gather.5.cloned.1.call-start = ((), (), s32[]{:S(2)}) async-start(), calls=%async_computation.2 | async-start | bytes 7864320 | tf_op jit(solution)/shard_map/all_gather | solution.py:17
  284.6 242.4 %copy-start = (f32[64,6144]{1,0:T(8,128)S(1)}, f32[64,6144]{1,0:T(8,128)}, u32[]{:S(2)}) copy-start(f32[64,6144]{1,0:T(8,128)} %get-tuple-element.7) | copy-start | bytes 4718596
  284.7 430.0 %all-reduce.5.cloned.1.call-start = ((), (), s32[]{:S(2)}) async-start(), calls=%async_computation.3 | async-start | bytes 131072 | tf_op jit(solution)/shard_map/psum | solution.py:18
  527.0 189.2 %copy-start.2 = (f32[64,256]{1,0:T(8,128)S(1)}, f32[64,256]{1,0:T(8,128)}, u32[]{:S(2)}) copy-start(f32[64,256]{1,0:T(8,128)} %all-reduce.3.cloned.1.call-done) | copy-start | bytes 196612
Sparse Core Ops, SparseCore 0:
  10.1 76.4 all-gather.2
  95.3 181.3 all-reduce.2
  284.8 63.6 all-gather.4
  535.7 178.9 all-reduce.4
where the time goes:
time: 724 us; the launch traced here: 723 us
  waiting for transfers between devices  439 us (61%)
  blocking collectives  242 us (33%)
  matrix products  25 us (3%)
  between operations  13.8 us (2%)
    psum x1, blocking collectives, per_device(): squares = lax.psum(jnp.sum(residual * residual, axis=1), 'rows')  242 us
    psum x1, waiting for transfers between devices, per_device(): coefficients = lax.psum(partial_value, 'rows')  181 us
    psum x1, waiting for transfers between devices, per_device(): gram = lax.psum(partial_gram, 'rows') / total_rows  179 us
    all_gather x1, waiting for transfers between devices, per_device(): panel = lax.all_gather(modes_basis, 'modes', axis=0, tiled=True)  78.7 us
    dot_general x3, matrix products, product(): jnp.dot(left, right, preferred_element_type=jnp.float32, precision=lax.Pr...  25 us
  transfers between devices with their start and end apart: 4, of which 3 were waited for; matrix products, arithmetic and copies ran while one was open for 0% of the time, Pallas kernels for 0%

commit v1 on v0

v1 whole, which is shorter than its diff:
```python
import functools

import jax
import jax.numpy as jnp
from jax import lax
from jax.experimental import pallas as pl
from jax.experimental.pallas import tpu as pltpu
from jax.sharding import PartitionSpec as P

MESH = pl.DeviceIdType.MESH
NX, NY, NZ = 4, 8, 8
CHUNKS = 3


def product(left, right, contract_right):
    return lax.dot_general(
        left,
        right,
        (((1,), (contract_right,)), ((), ())),
        precision=lax.Precision.HIGHEST,
        preferred_element_type=jnp.float32,
    )


def kernel(
    total_rows,
    phi_ref,
    s_ref,
    coef_ref,
    res_ref,
    gram_ref,
    norm_ref,
    phib,
    sb,
    rb,
    cpart,
    ccore,
    cx,
    cfirst,
    csecond,
    cfull,
    gpart,
    gcore,
    gx,
    gfirst,
    gsecond,
    gpair,
    csum,
    gsum,
    cmid,
    gmid,
    in_send,
    in_recv,
    own_sem,
    c_send,
    c_recv,
    g_send,
    g_recv,
    out_send,
    out_recv,
    out_own,
):
    block, local_cols = phi_ref.shape
    hub_cols = local_cols // NX
    width = hub_cols // CHUNKS
    half = block // 2
    quarter = half // 2

    rows = lax.axis_index("rows")
    x = lax.axis_index("modes")
    core = lax.rem(rows, 2)
    y = lax.rem(lax.div(rows, 2), NY)
    z = lax.div(rows, 2 * NY)

    def x_peer(d):
        return lax.rem(x + d, NX)

    def x_device(d):
        return (rows, x_peer(d))

    def y_device(d):
        return ((z * NY + lax.rem(y + d, NY)) * 2 + core, x)

    def z_device(d):
        return ((lax.rem(z + d, NZ) * NY + y) * 2 + core, x)

    sibling = ((z * NY + y) * 2 + (1 - core), x)

    barrier = pltpu.get_barrier_semaphore()
    for d in range(1, NX):
        pl.semaphore_signal(barrier, inc=1, device_id=x_device(d), device_id_type=MESH)
    for d in range(1, NY):
        pl.semaphore_signal(barrier, inc=1, device_id=y_device(d), device_id_type=MESH)
    for d in range(1, NZ):
        pl.semaphore_signal(barrier, inc=1, device_id=z_device(d), device_id_type=MESH)
    pl.semaphore_signal(barrier, inc=1, device_id=sibling, device_id_type=MESH)
    pl.semaphore_wait(barrier, (NX - 1) + (NY - 1) + (NZ - 1) + 1)

    pending = []

    def send(src, dst, ssem, rsem, device):
        copy = pltpu.make_async_remote_copy(
            src_ref=src, dst_ref=dst, send_sem=ssem, recv_sem=rsem, device_id=device, device_id_type=MESH
        )
        copy.start()
        pending.append(copy)
        return copy

    def block_rows(index):
        return pl.ds(pl.multiple_of(index * block, block), block)

    arrivals, own = [], []
    for k in range(CHUNKS):
        here = pl.ds(k * width, width)
        chunk_copies = []
        for d in (2, 1, 3):
            there = pl.ds(pl.multiple_of(x_peer(d) * hub_cols + k * width, 128), width)
            for i, (src, dst) in enumerate(((phi_ref, phib), (s_ref, sb))):
                chunk_copies.append(
                    send(
                        src.at[:, there],
                        dst.at[block_rows(x), here],
                        in_send.at[k, i, d - 1],
                        in_recv.at[k, i, d - 1],
                        x_device(d),
                    )
                )
        arrivals.append(chunk_copies)
        mine = pl.ds(pl.multiple_of(x * hub_cols + k * width, 128), width)
        own_copies = []
        for i, (src, dst) in enumerate(((phi_ref, phib), (s_ref, sb))):
            copy = pltpu.make_async_copy(src.at[:, mine], dst.at[block_rows(x), here], own_sem.at[k, i])
            copy.start()
            own_copies.append(copy)
        own.append(own_copies)

    acc = None
    for k in range(CHUNKS):
        for copy in own[k]:
            copy.wait()
        for copy in arrivals[k]:
            copy.wait_recv()
        here = pl.ds(k * width, width)
        term = product(sb[:, here], phib[:, here], 1)
        acc = term if acc is None else acc + term
    cpart[...] = acc.reshape(cpart.shape)

    def reduce_grid(part, from_core, from_x, mid, first, second, total, ssem, rsem):
        copy = send(part.at[:, 1 - core], from_core, ssem.at[0], rsem.at[0], sibling)
        copy.wait_recv()
        mid[...] = part[:, core] + from_core[...]
        copies = []
        for d in (2, 1, 3):
            copies.append(send(mid.at[x_peer(d)], from_x.at[x], ssem.at[d], rsem.at[d], x_device(d)))
        from_x[x] = mid[x]
        for copy in copies:
            copy.wait_recv()
        value = (from_x[0] + from_x[1]) + (from_x[2] + from_x[3])
        first[0, y] = value[:quarter]
        first[1, z] = value[quarter:]
        base = NX
        copies = []
        for d in (4, 3, 5, 2, 6, 1, 7):
            copies.append(
                send(first.at[0, y], first.at[0, y], ssem.at[base + d], rsem.at[base + d], y_device(d))
            )
            copies.append(
                send(first.at[1, z], first.at[1, z], ssem.at[base + 8 + d], rsem.at[base + 8 + d], z_device(d))
            )
        for copy in copies:
            copy.wait_recv()
        second[0, z] = jnp.sum(first[0], axis=0)
        second[1, y] = jnp.sum(first[1], axis=0)
        base = NX + 16
        copies = []
        for d in (4, 3, 5, 2, 6, 1, 7):
            copies.append(
                send(second.at[0, z], second.at[0, z], ssem.at[base + d], rsem.at[base + d], z_device(d))
            )
            copies.append(
                send(second.at[1, y], second.at[1, y], ssem.at[base + 8 + d], rsem.at[base + 8 + d], y_device(d))
            )
        for copy in copies:
            copy.wait_recv()
        total[:quarter] = jnp.sum(second[0], axis=0)
        total[quarter:] = jnp.sum(second[1], axis=0)

    reduce_grid(cpart, ccore, cx, cmid, cfirst, csecond, csum, c_send, c_recv)
    base = NX + 32
    copies = []
    for d in (2, 1, 3):
        copies.append(send(csum, cfull.at[core, x], c_send.at[base + d], c_recv.at[base + d], x_device(d)))
    cfull[core, x] = csum[...]
    for copy in copies:
        copy.wait_recv()
    copy = send(cfull.at[core], cfull.at[core], c_send.at[base], c_recv.at[base], sibling)
    copy.wait_recv()
    coef_ref[:half] = cfull[0, x]
    coef_ref[half:] = cfull[1, x]
    coefficients = jnp.concatenate(
        [cfull[c, a] for a in range(NX) for c in range(2)], axis=0
    )

    acc = None
    returns, own = [], []
    for k in range(CHUNKS):
        here = pl.ds(k * width, width)
        residual = sb[:, here] - product(coefficients, phib[:, here], 0)
        rb[:, here] = residual
        mine = pl.ds(pl.multiple_of(x * hub_cols + k * width, 128), width)
        for d in (2, 1, 3):
            returns.append(
                send(
                    rb.at[block_rows(x_peer(d)), here],
                    res_ref.at[:, mine],
                    out_send.at[k, d - 1],
                    out_recv.at[k, d - 1],
                    x_device(d),
                )
            )
        copy = pltpu.make_async_copy(rb.at[block_rows(x), here], res_ref.at[:, mine], out_own.at[k])
        copy.start()
        own.append(copy)
    for k in range(CHUNKS):
        here = pl.ds(k * width, width)
        residual = rb[:, here]
        term = product(residual, residual, 1)
        acc = term if acc is None else acc + term
    gpart[...] = acc.reshape(gpart.shape)

    reduce_grid(gpart, gcore, gx, gmid, gfirst, gsecond, gsum, g_send, g_recv)
    base = NX + 32
    gpair[core] = gsum[...]
    copy = send(gpair.at[core], gpair.at[core], g_send.at[base], g_recv.at[base], sibling)
    copy.wait_recv()
    gram = jnp.concatenate([gpair[0], gpair[1]], axis=0) / total_rows
    gram_ref[...] = gram
    column = lax.broadcasted_iota(jnp.int32, gram.shape, 1)
    row = lax.broadcasted_iota(jnp.int32, gram.shape, 0)
    diagonal = jnp.sum(jnp.where(column == row + x * block, gram, 0.0), axis=0, keepdims=True)
    diagonal = functools.reduce(jnp.add, [diagonal[:, a * block : (a + 1) * block] for a in range(NX)])
    norm_ref[...] = jnp.sqrt(diagonal)

    for copy in returns:
        copy.wait_recv()
    for copy in own:
        copy.wait()
    for copy in pending:
        copy.wait_send()


def per_device(modes_basis, snapshots):
    block, local_cols = modes_basis.shape
    size = block * NX
    hub_cols = local_cols // NX
    half, quarter = block // 2, block // 4
    total_rows = local_cols * lax.axis_size("rows")
    f32 = jnp.float32
    sems = NX + 32 + 4
    hbm = pl.BlockSpec(memory_space=pltpu.HBM)
    vmem = pl.BlockSpec(memory_space=pltpu.VMEM)
    part = pltpu.VMEM((NX, 2, half, size), f32)
    quad = pltpu.VMEM((NX, half, size), f32)
    ring = pltpu.VMEM((2, NY, quarter, size), f32)
    outs = pl.pallas_call(
        functools.partial(kernel, float(total_rows)),
        out_shape=(
            jax.ShapeDtypeStruct((block, size), f32),
            jax.ShapeDtypeStruct((block, local_cols), f32),
            jax.ShapeDtypeStruct((block, size), f32),
            jax.ShapeDtypeStruct((1, block), f32),
        ),
        in_specs=[hbm, hbm],
        out_specs=(vmem, hbm, vmem, vmem),
        scratch_shapes=[
            pltpu.VMEM((size, hub_cols), f32),
            pltpu.VMEM((size, hub_cols), f32),
            pltpu.VMEM((size, hub_cols), f32),
            part,
            quad,
            quad,
            ring,
            ring,
            pltpu.VMEM((2, NX, half, size), f32),
            part,
            quad,
            quad,
            ring,
            ring,
            pltpu.VMEM((2, half, size), f32),
            pltpu.VMEM((half, size), f32),
            pltpu.VMEM((half, size), f32),
            quad,
            quad,
            pltpu.SemaphoreType.DMA((CHUNKS, 2, NX - 1)),
            pltpu.SemaphoreType.DMA((CHUNKS, 2, NX - 1)),
            pltpu.SemaphoreType.DMA((CHUNKS, 2)),
            pltpu.SemaphoreType.DMA((sems,)),
            pltpu.SemaphoreType.DMA((sems,)),
            pltpu.SemaphoreType.DMA((sems,)),
            pltpu.SemaphoreType.DMA((sems,)),
            pltpu.SemaphoreType.DMA((CHUNKS, NX - 1)),
            pltpu.SemaphoreType.DMA((CHUNKS, NX - 1)),
            pltpu.SemaphoreType.DMA((CHUNKS,)),
        ],
        compiler_params=pltpu.CompilerParams(
            collective_id=0, has_side_effects=True, vmem_limit_bytes=56 * 1024 * 1024
        ),
        cost_estimate=pl.CostEstimate(
            flops=6 * size * size * hub_cols, bytes_accessed=12 * block * local_cols, transcendentals=0
        ),
    )(modes_basis, snapshots)
    coefficients, residual, gram, norm = outs
    return coefficients, residual, gram, norm.reshape(block)


def solution(mesh):
    in_specs = (P("modes", "rows"), P("modes", "rows"))
    out_specs = (P("modes", None), P("modes", "rows"), P("modes", None), P("modes"))
    return jax.shard_map(
        per_device, mesh=mesh, in_specs=in_specs, out_specs=out_specs, check_vma=False
    )
```

time: 724 us -> 115 us (0.16)
  waiting for transfers between devices: 439 us -> 0 us
  blocking collectives: 242 us -> 0 us
  Pallas kernels: 0 us -> 109 us
  matrix products: 25 us -> 0 us
  between operations: 13.8 us -> 0.64 us
    psum x2 -> x0, waiting for transfers between devices: 360 us -> none  [the longest x1 181 us: per_device(): coefficients = lax.psum(partial_value, 'rows')]
    psum x1 -> x0, blocking collectives: 242 us -> none  [per_device(): squares = lax.psum(jnp.sum(residual * residual, axis=1), 'rows')]
    pallas_call x0 -> x1, Pallas kernels: none -> 109 us  [per_device(): pl.pallas_call(functools.partial(kernel, float(total_rows)), out_shape=(j...]
    all_gather x2 -> x0, waiting for transfers between devices: 78.7 us -> none  [the longest x1 78.7 us: per_device(): panel = lax.all_gather(modes_basis, 'modes', axis=0, tiled=True)]
    dot_general x3 -> x0, matrix products: 25 us -> none  [product(): jnp.dot(left, right, preferred_element_type=jnp.float32, precision=lax.Pr...]
  transfers between devices with their start and end apart: 4 -> 0, of which waited for: 3 -> 0; matrix products, arithmetic and copies ran while one was open for 0% -> 0% of each run, Pallas kernels for 0% -> 0%
where the time goes in v1:
time: 115 us
  Pallas kernels  109 us (95%)
  local copies, waits for them, and re-layouts  5.32 us (5%)
    pallas_call x1, Pallas kernels, per_device(): pl.pallas_call(functools.partial(kernel, float(total_rows)), out_shape=(j...  109 us
    unnamed x8, local copies, waits for them, and re-layouts  5.32 us

profile of v1, /device:TPU:1, one launch (start us, length us, event | category | flops | bytes accessed | tf_op | source)
XLA Modules:
  0.0 115.1 jit_solution(11120872059530452226)
XLA Ops:
  0.6 109.1 %shard_map.57 = (f32[64,256]{1,0:T(8,128)}, f32[64,6144]{1,0:T(8,128)}, f32[64,256]{1,0:T(8,128)}, f32[1,64]{1,0:T(1,128)}) custom-call(f32[64,6144]{1,0:T(8,128)} %phi_ref.1, f32[64,6144]{1,0:T(8,128)} %s_ref.1), custom_call_target="tpu_custom_call" | custom-call | flops 603979776 | bytes 4718592 | tf_op jit(solution)/shard_map/pallas_call | solution.py:265
  109.8 1.5 %copy.10 = f32[64,256]{1,0:T(8,128)} copy(f32[64,256]{1,0:T(8,128)} %get-tuple-element.16) | data formatting | bytes 131072
  111.2 0.0 copy-start
  111.3 0.0 copy-start.1
  111.3 2.7 %copy.11 = f32[64,6144]{1,0:T(8,128)} copy(f32[64,6144]{1,0:T(8,128)} %get-tuple-element.17) | data formatting | bytes 3145728
  113.9 0.0 copy-done
  114.0 0.6 copy.12
  114.6 0.0 copy-done.1
  114.6 0.5 copy.13
Async XLA Ops:
  111.2 2.7 %copy-start = (f32[64,256]{1,0:T(8,128)S(1)}, f32[64,256]{1,0:T(8,128)}, u32[]{:S(2)}) copy-start(f32[64,256]{1,0:T(8,128)} %get-tuple-element.18) | copy-start | bytes 196612
  111.3 3.3 %copy-start.1 = (f32[1,64]{1,0:T(1,128)S(1)}, f32[1,64]{1,0:T(1,128)}, u32[]{:S(2)}) copy-start(f32[1,64]{1,0:T(1,128)} %get-tuple-element.11) | copy-start | bytes 772

commit v2 on v1

--- a/solution.py
+++ b/solution.py
@@ -10,6 +10,8 @@
 MESH = pl.DeviceIdType.MESH
 NX, NY, NZ = 4, 8, 8
 CHUNKS = 3
+PIECES = 6
+EARLY = 1
 
 
 def product(left, right, contract_right):
@@ -20,6 +22,10 @@
         precision=lax.Precision.HIGHEST,
         preferred_element_type=jnp.float32,
     )
+
+
+def plain_product(left, right):
+    return lax.dot_general(left, right, (((1,), (1,)), ((), ())), preferred_element_type=jnp.float32)
 
 
 def kernel(
@@ -87,12 +93,11 @@
     sibling = ((z * NY + y) * 2 + (1 - core), x)
 
     barrier = pltpu.get_barrier_semaphore()
-    for d in range(1, NX):
+    for d in (4, 3, 5, 2, 6, 1, 7):
+        pl.semaphore_signal(barrier, inc=1, device_id=y_device(d), device_id_type=MESH)
+        pl.semaphore_signal(barrier, inc=1, device_id=z_device(d), device_id_type=MESH)
+    for d in (2, 1, 3):
         pl.semaphore_signal(barrier, inc=1, device_id=x_device(d), device_id_type=MESH)
-    for d in range(1, NY):
-        pl.semaphore_signal(barrier, inc=1, device_id=y_device(d), device_id_type=MESH)
-    for d in range(1, NZ):
-        pl.semaphore_signal(barrier, inc=1, device_id=z_device(d), device_id_type=MESH)
     pl.semaphore_signal(barrier, inc=1, device_id=sibling, device_id_type=MESH)
     pl.semaphore_wait(barrier, (NX - 1) + (NY - 1) + (NZ - 1) + 1)
 
@@ -145,7 +150,7 @@
         acc = term if acc is None else acc + term
     cpart[...] = acc.reshape(cpart.shape)
 
-    def reduce_grid(part, from_core, from_x, mid, first, second, total, ssem, rsem):
+    def reduce_grid(part, from_core, from_x, mid, first, second, total, ssem, rsem, meanwhile):
         copy = send(part.at[:, 1 - core], from_core, ssem.at[0], rsem.at[0], sibling)
         copy.wait_recv()
         mid[...] = part[:, core] + from_core[...]
@@ -155,6 +160,7 @@
         from_x[x] = mid[x]
         for copy in copies:
             copy.wait_recv()
+        meanwhile()
         value = (from_x[0] + from_x[1]) + (from_x[2] + from_x[3])
         first[0, y] = value[:quarter]
         first[1, z] = value[quarter:]
@@ -185,50 +191,77 @@
         total[:quarter] = jnp.sum(second[0], axis=0)
         total[quarter:] = jnp.sum(second[1], axis=0)
 
-    reduce_grid(cpart, ccore, cx, cmid, cfirst, csecond, csum, c_send, c_recv)
+    reduce_grid(cpart, ccore, cx, cmid, cfirst, csecond, csum, c_send, c_recv, lambda: None)
     base = NX + 32
+    cfull[core, x] = csum[...]
     copies = []
     for d in (2, 1, 3):
-        copies.append(send(csum, cfull.at[core, x], c_send.at[base + d], c_recv.at[base + d], x_device(d)))
-    cfull[core, x] = csum[...]
-    for copy in copies:
+        copies.append((d, send(csum, cfull.at[core, x], c_send.at[base + d], c_recv.at[base + d], x_device(d))))
+    passed = [send(csum, cfull.at[core, x], c_send.at[base], c_recv.at[base], sibling)]
+    for d, copy in copies[1:] + copies[:1]:
         copy.wait_recv()
-    copy = send(cfull.at[core], cfull.at[core], c_send.at[base], c_recv.at[base], sibling)
-    copy.wait_recv()
+        origin = lax.rem(x + NX - d, NX)
+        passed.append(
+            send(
+                cfull.at[core, origin],
+                cfull.at[core, origin],
+                c_send.at[base + NX + d],
+                c_recv.at[base + NX + d],
+                sibling,
+            )
+        )
+    for copy in passed:
+        copy.wait_recv()
     coef_ref[:half] = cfull[0, x]
     coef_ref[half:] = cfull[1, x]
     coefficients = jnp.concatenate(
         [cfull[c, a] for a in range(NX) for c in range(2)], axis=0
     )
 
-    acc = None
     returns, own = [], []
-    for k in range(CHUNKS):
-        here = pl.ds(k * width, width)
-        residual = sb[:, here] - product(coefficients, phib[:, here], 0)
-        rb[:, here] = residual
-        mine = pl.ds(pl.multiple_of(x * hub_cols + k * width, 128), width)
+    piece = hub_cols // PIECES
+
+    def give_back(index):
+        here = pl.ds(index * piece, piece)
+        mine = pl.ds(pl.multiple_of(x * hub_cols + index * piece, 128), piece)
         for d in (2, 1, 3):
             returns.append(
                 send(
                     rb.at[block_rows(x_peer(d)), here],
                     res_ref.at[:, mine],
-                    out_send.at[k, d - 1],
-                    out_recv.at[k, d - 1],
+                    out_send.at[index, d - 1],
+                    out_recv.at[index, d - 1],
                     x_device(d),
                 )
             )
-        copy = pltpu.make_async_copy(rb.at[block_rows(x), here], res_ref.at[:, mine], out_own.at[k])
-        copy.start()
-        own.append(copy)
+
+    sent = 0
     for k in range(CHUNKS):
         here = pl.ds(k * width, width)
-        residual = rb[:, here]
-        term = product(residual, residual, 1)
-        acc = term if acc is None else acc + term
-    gpart[...] = acc.reshape(gpart.shape)
-
-    reduce_grid(gpart, gcore, gx, gmid, gfirst, gsecond, gsum, g_send, g_recv)
+        rb[:, here] = sb[:, here] - product(coefficients, phib[:, here], 0)
+        while sent < EARLY and (sent + 1) * piece <= (k + 1) * width:
+            give_back(sent)
+            sent += 1
+    mine = pl.ds(pl.multiple_of(x * hub_cols, 128), hub_cols)
+    copy = pltpu.make_async_copy(rb.at[block_rows(x)], res_ref.at[:, mine], out_own)
+    copy.start()
+    own.append(copy)
+    same = cross = None
+    for k in range(CHUNKS):
+        residual = rb[:, pl.ds(k * width, width)]
+        high = residual.astype(jnp.bfloat16)
+        low = (residual - high.astype(jnp.float32)).astype(jnp.bfloat16)
+        high_high = plain_product(high, high)
+        high_low = plain_product(high, low)
+        same = high_high if same is None else same + high_high
+        cross = high_low if cross is None else cross + high_low
+    gpart[...] = (same + (cross + cross.T)).reshape(gpart.shape)
+
+    def send_the_rest():
+        for index in range(EARLY, PIECES):
+            give_back(index)
+
+    reduce_grid(gpart, gcore, gx, gmid, gfirst, gsecond, gsum, g_send, g_recv, send_the_rest)
     base = NX + 32
     gpair[core] = gsum[...]
     copy = send(gpair.at[core], gpair.at[core], g_send.at[base], g_recv.at[base], sibling)
@@ -249,6 +282,28 @@
         copy.wait_send()
 
 
+def copy_kernel(*refs):
+    n = (len(refs) - 1) // 2
+    sems = refs[-1]
+    copies = [pltpu.make_async_copy(refs[i], refs[n + i], sems.at[i]) for i in range(n)]
+    for copy in copies:
+        copy.start()
+    for copy in copies:
+        copy.wait()
+
+
+def copied(arrays):
+    hbm = pl.BlockSpec(memory_space=pltpu.HBM)
+    return pl.pallas_call(
+        copy_kernel,
+        out_shape=tuple(jax.ShapeDtypeStruct(a.shape, a.dtype) for a in arrays),
+        in_specs=[hbm] * len(arrays),
+        out_specs=(hbm,) * len(arrays),
+        scratch_shapes=[pltpu.SemaphoreType.DMA((len(arrays),))],
+        compiler_params=pltpu.CompilerParams(vmem_limit_bytes=56 * 1024 * 1024),
+    )(*arrays)
+
+
 def per_device(modes_basis, snapshots):
     block, local_cols = modes_basis.shape
     size = block * NX
@@ -256,7 +311,7 @@
     half, quarter = block // 2, block // 4
     total_rows = local_cols * lax.axis_size("rows")
     f32 = jnp.float32
-    sems = NX + 32 + 4
+    sems = NX + 32 + 2 * NX
     hbm = pl.BlockSpec(memory_space=pltpu.HBM)
     vmem = pl.BlockSpec(memory_space=pltpu.VMEM)
     part = pltpu.VMEM((NX, 2, half, size), f32)
@@ -299,9 +354,9 @@
             pltpu.SemaphoreType.DMA((sems,)),
             pltpu.SemaphoreType.DMA((sems,)),
             pltpu.SemaphoreType.DMA((sems,)),
-            pltpu.SemaphoreType.DMA((CHUNKS, NX - 1)),
-            pltpu.SemaphoreType.DMA((CHUNKS, NX - 1)),
-            pltpu.SemaphoreType.DMA((CHUNKS,)),
+            pltpu.SemaphoreType.DMA((PIECES, NX - 1)),
+            pltpu.SemaphoreType.DMA((PIECES, NX - 1)),
+            pltpu.SemaphoreType.DMA,
         ],
         compiler_params=pltpu.CompilerParams(
             collective_id=0, has_side_effects=True, vmem_limit_bytes=56 * 1024 * 1024
@@ -310,7 +365,7 @@
             flops=6 * size * size * hub_cols, bytes_accessed=12 * block * local_cols, transcendentals=0
         ),
     )(modes_basis, snapshots)
-    coefficients, residual, gram, norm = outs
+    coefficients, residual, gram, norm = copied(outs)
     return coefficients, residual, gram, norm.reshape(block)
 
 

time: 115 us -> 151 us (1.31); the launches traced: 115 us -> 150 us
  Pallas kernels: 109 us -> 149 us
  local copies, waits for them, and re-layouts: 5.32 us -> 0 us
    pallas_call x0 -> x1, Pallas kernels: none -> 52.8 us  [copied(): pl.pallas_call(copy_kernel, out_shape=tuple((jax.ShapeDtypeStruct(a.shape...]
    pallas_call x1, Pallas kernels: 109 us -> 96.1 us  [per_device(): pl.pallas_call(functools.partial(kernel, float(total_rows)), out_shape=(j...]
    unnamed x8 -> x0, local copies, waits for them, and re-layouts: 5.32 us -> none
where the time goes in v2:
time: 151 us; the launch traced here: 150 us
  Pallas kernels  149 us (99%)
    pallas_call x1, Pallas kernels, per_device(): pl.pallas_call(functools.partial(kernel, float(total_rows)), out_shape=(j...  96.1 us
    pallas_call x1, Pallas kernels, copied(): pl.pallas_call(copy_kernel, out_shape=tuple((jax.ShapeDtypeStruct(a.shape...  52.8 us

profile of v2, /device:TPU:1, one launch (start us, length us, event | category | flops | bytes accessed | tf_op | source)
XLA Modules:
  0.0 149.5 jit_solution(7522997163616511680)
XLA Ops:
  0.6 96.1 %shard_map.57 = (f32[64,256]{1,0:T(8,128)}, f32[64,6144]{1,0:T(8,128)}, f32[64,256]{1,0:T(8,128)}, f32[1,64]{1,0:T(1,128)}) custom-call(f32[64,6144]{1,0:T(8,128)} %phi_ref.1, f32[64,6144]{1,0:T(8,128)} %s_ref.1), custom_call_target="tpu_custom_call" | custom-call | flops 603979776 | bytes 4718592 | tf_op jit(solution)/shard_map/pallas_call | solution.py:320
  96.7 52.8 %shard_map.58 = (f32[64,256]{1,0:T(8,128)}, f32[64,6144]{1,0:T(8,128)}, f32[64,256]{1,0:T(8,128)}, f32[1,64]{1,0:T(1,128)}) custom-call(f32[64,256]{1,0:T(8,128)} %get-tuple-element.12.refs_0_, f32[64,6144]{1,0:T(8,128)} %get-tuple-element.13.refs_1_, f32[64,256]{1,0:T(8,128)} %get-tuple-element.14.refs_2_, f32[1,64]{1,0:T(1,128)} %get-tuple-element.15.refs_3_), custom_call_target="tpu_custom_call" | custom-call | tf_op jit(solution)/shard_map/pallas_call | solution.py:297

commit v3 on v2

--- a/solution.py
+++ b/solution.py
@@ -294,13 +294,13 @@
 
 def copied(arrays):
     hbm = pl.BlockSpec(memory_space=pltpu.HBM)
+    vmem = pl.BlockSpec(memory_space=pltpu.VMEM)
     return pl.pallas_call(
         copy_kernel,
         out_shape=tuple(jax.ShapeDtypeStruct(a.shape, a.dtype) for a in arrays),
-        in_specs=[hbm] * len(arrays),
+        in_specs=[vmem] * len(arrays),
         out_specs=(hbm,) * len(arrays),
         scratch_shapes=[pltpu.SemaphoreType.DMA((len(arrays),))],
-        compiler_params=pltpu.CompilerParams(vmem_limit_bytes=56 * 1024 * 1024),
     )(*arrays)
 
 
@@ -320,13 +320,13 @@
     outs = pl.pallas_call(
         functools.partial(kernel, float(total_rows)),
         out_shape=(
-            jax.ShapeDtypeStruct((block, size), f32),
-            jax.ShapeDtypeStruct((block, local_cols), f32),
-            jax.ShapeDtypeStruct((block, size), f32),
-            jax.ShapeDtypeStruct((1, block), f32),
+            pltpu.VMEM((block, size), f32),
+            pltpu.VMEM((block, local_cols), f32),
+            pltpu.VMEM((block, size), f32),
+            pltpu.VMEM((1, block), f32),
         ),
         in_specs=[hbm, hbm],
-        out_specs=(vmem, hbm, vmem, vmem),
+        out_specs=(vmem, vmem, vmem, vmem),
         scratch_shapes=[
             pltpu.VMEM((size, hub_cols), f32),
             pltpu.VMEM((size, hub_cols), f32),

time: 151 us -> 103 us (0.68)
  Pallas kernels: 149 us -> 98.2 us
  local copies, waits for them, and re-layouts: 0 us -> 2.98 us
    pallas_call x1, Pallas kernels: 52.8 us -> 2.61 us  [copied(): pl.pallas_call(copy_kernel, out_shape=tuple((jax.ShapeDtypeStruct(a.shape...]
    unnamed x0 -> x8, local copies, waits for them, and re-layouts: none -> 2.98 us
where the time goes in v3:
time: 103 us; the launch traced here: 102 us
  Pallas kernels  98.2 us (95%)
  local copies, waits for them, and re-layouts  2.98 us (3%)
    pallas_call x1, Pallas kernels, per_device(): pl.pallas_call(functools.partial(kernel, float(total_rows)), out_shape=(p...  95.6 us
    unnamed x8, local copies, waits for them, and re-layouts  2.98 us
    pallas_call x1, Pallas kernels, copied(): pl.pallas_call(copy_kernel, out_shape=tuple((jax.ShapeDtypeStruct(a.shape...  2.61 us

profile of v3, /device:TPU:1, one launch (start us, length us, event | category | flops | bytes accessed | tf_op | source)
XLA Modules:
  0.0 101.8 jit_solution(13174317670482290856)
XLA Ops:
  0.6 95.6 %shard_map.57 = (f32[64,256]{1,0:T(8,128)S(1)}, f32[64,6144]{1,0:T(8,128)S(1)}, f32[64,256]{1,0:T(8,128)S(1)}, f32[1,64]{1,0:T(1,128)S(1)}) custom-call(f32[64,6144]{1,0:T(8,128)} %phi_ref.1, f32[64,6144]{1,0:T(8,128)} %s_ref.1), custom_call_target="tpu_custom_call" | custom-call | flops 603979776 | bytes 4718592 | tf_op jit(solution)/shard_map/pallas_call | solution.py:320
  96.2 0.0 copy-start
  96.2 1.1 %copy-done = f32[64,6144]{1,0:T(8,128)} copy-done((f32[64,6144]{1,0:T(8,128)}, f32[64,6144]{1,0:T(8,128)S(1)}, u32[]{:S(2)}) %copy-start) | copy-done | bytes 1572888
  97.4 0.0 copy-start.1
  97.4 0.6 copy-done.1
  98.0 0.0 copy-start.2
  98.0 0.6 copy-done.2
  98.6 0.0 copy-start.3
  98.6 0.6 copy-done.3
  99.2 2.6 %shard_map.58 = (f32[64,256]{1,0:T(8,128)}, f32[64,6144]{1,0:T(8,128)}, f32[64,256]{1,0:T(8,128)}, f32[1,64]{1,0:T(1,128)}) custom-call(f32[64,256]{1,0:T(8,128)} %copy-done.1, f32[64,6144]{1,0:T(8,128)} %copy-done, f32[64,256]{1,0:T(8,128)} %copy-done.2, f32[1,64]{1,0:T(1,128)} %copy-done.3), custom_call_target="tpu_custom_call" | custom-call | tf_op jit(solution)/shard_map/pallas_call | solution.py:298
Async XLA Ops:
  96.2 1.2 %copy-start = (f32[64,6144]{1,0:T(8,128)}, f32[64,6144]{1,0:T(8,128)S(1)}, u32[]{:S(2)}) copy-start(f32[64,6144]{1,0:T(8,128)S(1)} %get-tuple-element.13.refs_1_) | copy-start | bytes 4718596
  97.4 0.6 copy-start.1
  98.0 0.6 copy-start.2
  98.6 0.6 copy-start.3

commit v4 on v3

--- a/solution.py
+++ b/solution.py
@@ -12,6 +12,7 @@
 CHUNKS = 3
 PIECES = 6
 EARLY = 1
+MIDDLE = 2
 
 
 def product(left, right, contract_right):
@@ -158,9 +159,10 @@
         for d in (2, 1, 3):
             copies.append(send(mid.at[x_peer(d)], from_x.at[x], ssem.at[d], rsem.at[d], x_device(d)))
         from_x[x] = mid[x]
+        meanwhile[0]()
         for copy in copies:
             copy.wait_recv()
-        meanwhile()
+        meanwhile[1]()
         value = (from_x[0] + from_x[1]) + (from_x[2] + from_x[3])
         first[0, y] = value[:quarter]
         first[1, z] = value[quarter:]
@@ -191,7 +193,7 @@
         total[:quarter] = jnp.sum(second[0], axis=0)
         total[quarter:] = jnp.sum(second[1], axis=0)
 
-    reduce_grid(cpart, ccore, cx, cmid, cfirst, csecond, csum, c_send, c_recv, lambda: None)
+    reduce_grid(cpart, ccore, cx, cmid, cfirst, csecond, csum, c_send, c_recv, (lambda: None, lambda: None))
     base = NX + 32
     cfull[core, x] = csum[...]
     copies = []
@@ -257,11 +259,17 @@
         cross = high_low if cross is None else cross + high_low
     gpart[...] = (same + (cross + cross.T)).reshape(gpart.shape)
 
+    def send_some():
+        for index in range(EARLY, MIDDLE):
+            give_back(index)
+
     def send_the_rest():
-        for index in range(EARLY, PIECES):
+        for index in range(MIDDLE, PIECES):
             give_back(index)
 
-    reduce_grid(gpart, gcore, gx, gmid, gfirst, gsecond, gsum, g_send, g_recv, send_the_rest)
+    reduce_grid(
+        gpart, gcore, gx, gmid, gfirst, gsecond, gsum, g_send, g_recv, (send_some, send_the_rest)
+    )
     base = NX + 32
     gpair[core] = gsum[...]
     copy = send(gpair.at[core], gpair.at[core], g_send.at[base], g_recv.at[base], sibling)
@@ -301,6 +309,7 @@
         in_specs=[vmem] * len(arrays),
         out_specs=(hbm,) * len(arrays),
         scratch_shapes=[pltpu.SemaphoreType.DMA((len(arrays),))],
+        compiler_params=pltpu.CompilerParams(vmem_limit_bytes=1024 * 1024),
     )(*arrays)
 
 

time: 103 us -> 98.2 us (0.953); the launches traced: 102 us -> 98.1 us
  local copies, waits for them, and re-layouts: 2.98 us -> 0 us
    unnamed x8 -> x0, local copies, waits for them, and re-layouts: 2.98 us -> none
    pallas_call x1, Pallas kernels: 2.61 us -> 1.21 us  [copied(): pl.pallas_call(copy_kernel, out_shape=tuple((jax.ShapeDtypeStruct(a.shape...]
where the time goes in v4:
time: 98.2 us; the launch traced here: 98.1 us
  Pallas kernels  97.4 us (99%)
    pallas_call x1, Pallas kernels, per_device(): pl.pallas_call(functools.partial(kernel, float(total_rows)), out_shape=(p...  96.2 us

profile of v4, /device:TPU:1, one launch (start us, length us, event | category | flops | bytes accessed | tf_op | source)
XLA Modules:
  0.0 98.1 jit_solution(14830577879189029130)
XLA Ops:
  0.6 96.2 %shard_map.57 = (f32[64,256]{1,0:T(8,128)S(1)}, f32[64,6144]{1,0:T(8,128)S(1)}, f32[64,256]{1,0:T(8,128)S(1)}, f32[1,64]{1,0:T(1,128)S(1)}) custom-call(f32[64,6144]{1,0:T(8,128)} %phi_ref.1, f32[64,6144]{1,0:T(8,128)} %s_ref.1), custom_call_target="tpu_custom_call" | custom-call | flops 603979776 | bytes 4718592 | tf_op jit(solution)/shard_map/pallas_call | solution.py:329
  96.9 1.2 %shard_map.58 = (f32[64,256]{1,0:T(8,128)}, f32[64,6144]{1,0:T(8,128)}, f32[64,256]{1,0:T(8,128)}, f32[1,64]{1,0:T(1,128)}) custom-call(f32[64,256]{1,0:T(8,128)S(1)} %get-tuple-element.12.refs_0_, f32[64,6144]{1,0:T(8,128)S(1)} %get-tuple-element.13.refs_1_, f32[64,256]{1,0:T(8,128)S(1)} %get-tuple-element.14.refs_2_, f32[1,64]{1,0:T(1,128)S(1)} %get-tuple-element.15.refs_3_), custom_call_target="tpu_custom_call" | custom-call | tf_op jit(solution)/shard_map/pallas_call | solution.py:306

commit v5 on v4

--- a/solution.py
+++ b/solution.py
@@ -9,10 +9,12 @@
 
 MESH = pl.DeviceIdType.MESH
 NX, NY, NZ = 4, 8, 8
-CHUNKS = 3
+CHUNKS = 6
+WINDOW = 4
+PARTS = 3
 PIECES = 6
 EARLY = 1
-MIDDLE = 2
+MIDDLE = 1
 
 
 def product(left, right, contract_right):
@@ -66,6 +68,11 @@
     out_send,
     out_recv,
     out_own,
+    phi_last,
+    s_last,
+    last_send,
+    last_recv,
+    last_own,
 ):
     block, local_cols = phi_ref.shape
     hub_cols = local_cols // NX
@@ -112,11 +119,18 @@
         pending.append(copy)
         return copy
 
+    def settle(keep):
+        done = pending[: len(pending) - keep]
+        del pending[: len(done)]
+        for copy in done:
+            copy.wait_send()
+
     def block_rows(index):
         return pl.ds(pl.multiple_of(index * block, block), block)
 
     arrivals, own = [], []
-    for k in range(CHUNKS):
+
+    def fetch(k):
         here = pl.ds(k * width, width)
         chunk_copies = []
         for d in (2, 1, 3):
@@ -140,12 +154,17 @@
             own_copies.append(copy)
         own.append(own_copies)
 
+    for k in range(WINDOW):
+        fetch(k)
+
     acc = None
     for k in range(CHUNKS):
         for copy in own[k]:
             copy.wait()
         for copy in arrivals[k]:
             copy.wait_recv()
+        if k + WINDOW < CHUNKS:
+            fetch(k + WINDOW)
         here = pl.ds(k * width, width)
         term = product(sb[:, here], phib[:, here], 1)
         acc = term if acc is None else acc + term
@@ -175,6 +194,7 @@
             copies.append(
                 send(first.at[1, z], first.at[1, z], ssem.at[base + 8 + d], rsem.at[base + 8 + d], z_device(d))
             )
+        meanwhile[2]()
         for copy in copies:
             copy.wait_recv()
         second[0, z] = jnp.sum(first[0], axis=0)
@@ -188,12 +208,55 @@
             copies.append(
                 send(second.at[1, y], second.at[1, y], ssem.at[base + 8 + d], rsem.at[base + 8 + d], y_device(d))
             )
+        meanwhile[3]()
         for copy in copies:
             copy.wait_recv()
         total[:quarter] = jnp.sum(second[0], axis=0)
         total[quarter:] = jnp.sum(second[1], axis=0)
 
-    reduce_grid(cpart, ccore, cx, cmid, cfirst, csecond, csum, c_send, c_recv, (lambda: None, lambda: None))
+    piece = hub_cols // PIECES
+    last = (PIECES - 1) * piece
+    extra = []
+
+    def nothing():
+        pass
+
+    def gather_last():
+        for e in (2, 1, 3):
+            for d in range(1, NX):
+                owner = lax.rem(x + e + d, NX)
+                there = pl.ds(pl.multiple_of(owner * hub_cols + last, 128), piece)
+                extra.append(
+                    send(
+                        phi_ref.at[:, there],
+                        phi_last.at[d - 1, block_rows(x)],
+                        last_send.at[e - 1, d - 1],
+                        last_recv.at[e - 1, d - 1],
+                        x_device(e),
+                    )
+                )
+
+    extra_own = []
+    for d in range(1, NX):
+        there = pl.ds(pl.multiple_of(x_peer(d) * hub_cols + last, 128), piece)
+        pairs = ((phi_ref.at[:, there], phi_last.at[d - 1, block_rows(x)]), (s_ref.at[:, there], s_last.at[d - 1]))
+        for i, (src, dst) in enumerate(pairs):
+            copy = pltpu.make_async_copy(src, dst, last_own.at[i, d - 1])
+            copy.start()
+            extra_own.append(copy)
+
+    reduce_grid(
+        cpart,
+        ccore,
+        cx,
+        cmid,
+        cfirst,
+        csecond,
+        csum,
+        c_send,
+        c_recv,
+        (nothing, gather_last, lambda: settle((NY - 1) + (NZ - 1) + (NX - 1) ** 2), nothing),
+    )
     base = NX + 32
     cfull[core, x] = csum[...]
     copies = []
@@ -221,7 +284,6 @@
     )
 
     returns, own = [], []
-    piece = hub_cols // PIECES
 
     def give_back(index):
         here = pl.ds(index * piece, piece)
@@ -238,19 +300,15 @@
             )
 
     sent = 0
-    for k in range(CHUNKS):
+    same = cross = None
+    width = hub_cols // PARTS
+    for k in range(PARTS):
         here = pl.ds(k * width, width)
-        rb[:, here] = sb[:, here] - product(coefficients, phib[:, here], 0)
+        residual = sb[:, here] - product(coefficients, phib[:, here], 0)
+        rb[:, here] = residual
         while sent < EARLY and (sent + 1) * piece <= (k + 1) * width:
             give_back(sent)
             sent += 1
-    mine = pl.ds(pl.multiple_of(x * hub_cols, 128), hub_cols)
-    copy = pltpu.make_async_copy(rb.at[block_rows(x)], res_ref.at[:, mine], out_own)
-    copy.start()
-    own.append(copy)
-    same = cross = None
-    for k in range(CHUNKS):
-        residual = rb[:, pl.ds(k * width, width)]
         high = residual.astype(jnp.bfloat16)
         low = (residual - high.astype(jnp.float32)).astype(jnp.bfloat16)
         high_high = plain_product(high, high)
@@ -264,11 +322,36 @@
             give_back(index)
 
     def send_the_rest():
-        for index in range(MIDDLE, PIECES):
+        mine = pl.ds(pl.multiple_of(x * hub_cols, 128), hub_cols)
+        copy = pltpu.make_async_copy(rb.at[block_rows(x)], res_ref.at[:, mine], out_own)
+        copy.start()
+        own.append(copy)
+        for index in range(MIDDLE, PIECES - 1):
             give_back(index)
 
+    def own_residual():
+        for copy in extra_own:
+            copy.wait()
+        for copy in extra:
+            copy.wait_recv()
+        mine = jnp.concatenate([cfull[0, x], cfull[1, x]], axis=0)
+        for d in range(1, NX):
+            there = pl.ds(pl.multiple_of(x_peer(d) * hub_cols + last, 128), piece)
+            res_ref[:, there] = s_last[d - 1] - product(mine, phi_last[d - 1], 0)
+
+    later = (NX - 1) * (PIECES - 1) + (NY - 1) + (NZ - 1)
+
     reduce_grid(
-        gpart, gcore, gx, gmid, gfirst, gsecond, gsum, g_send, g_recv, (send_some, send_the_rest)
+        gpart,
+        gcore,
+        gx,
+        gmid,
+        gfirst,
+        gsecond,
+        gsum,
+        g_send,
+        g_recv,
+        (send_some, send_the_rest, own_residual, lambda: settle(later + (NY - 1) + (NZ - 1))),
     )
     base = NX + 32
     gpair[core] = gsum[...]
@@ -286,8 +369,7 @@
         copy.wait_recv()
     for copy in own:
         copy.wait()
-    for copy in pending:
-        copy.wait_send()
+    settle(0)
 
 
 def copy_kernel(*refs):
@@ -366,6 +448,11 @@
             pltpu.SemaphoreType.DMA((PIECES, NX - 1)),
             pltpu.SemaphoreType.DMA((PIECES, NX - 1)),
             pltpu.SemaphoreType.DMA,
+            pltpu.VMEM((NX - 1, size, hub_cols // PIECES), f32),
+            pltpu.VMEM((NX - 1, block, hub_cols // PIECES), f32),
+            pltpu.SemaphoreType.DMA((NX - 1, NX - 1)),
+            pltpu.SemaphoreType.DMA((NX - 1, NX - 1)),
+            pltpu.SemaphoreType.DMA((2, NX - 1)),
         ],
         compiler_params=pltpu.CompilerParams(
             collective_id=0, has_side_effects=True, vmem_limit_bytes=56 * 1024 * 1024

time: 98.2 us -> 96.7 us (0.985)
  Pallas kernels: 97.4 us -> 95.9 us
    pallas_call x1, Pallas kernels: 96.2 us -> 94.7 us  [per_device(): pl.pallas_call(functools.partial(kernel, float(total_rows)), out_shape=(p...]
where the time goes in v5:
time: 96.7 us; the launch traced here: 96.6 us
  Pallas kernels  95.9 us (99%)
    pallas_call x1, Pallas kernels, per_device(): pl.pallas_call(functools.partial(kernel, float(total_rows)), out_shape=(p...  94.7 us

profile of v5, /device:TPU:1, one launch (start us, length us, event | category | flops | bytes accessed | tf_op | source)
XLA Modules:
  0.0 96.6 jit_solution(17856177634924405892)
XLA Ops:
  0.6 94.7 %shard_map.57 = (f32[64,256]{1,0:T(8,128)S(1)}, f32[64,6144]{1,0:T(8,128)S(1)}, f32[64,256]{1,0:T(8,128)S(1)}, f32[1,64]{1,0:T(1,128)S(1)}) custom-call(f32[64,6144]{1,0:T(8,128)} %phi_ref.1, f32[64,6144]{1,0:T(8,128)} %s_ref.1), custom_call_target="tpu_custom_call" | custom-call | flops 603979776 | bytes 4718592 | tf_op jit(solution)/shard_map/pallas_call | solution.py:411
  95.4 1.2 %shard_map.58 = (f32[64,256]{1,0:T(8,128)}, f32[64,6144]{1,0:T(8,128)}, f32[64,256]{1,0:T(8,128)}, f32[1,64]{1,0:T(1,128)}) custom-call(f32[64,256]{1,0:T(8,128)S(1)} %get-tuple-element.12.refs_0_, f32[64,6144]{1,0:T(8,128)S(1)} %get-tuple-element.13.refs_1_, f32[64,256]{1,0:T(8,128)S(1)} %get-tuple-element.14.refs_2_, f32[1,64]{1,0:T(1,128)S(1)} %get-tuple-element.15.refs_3_), custom_call_target="tpu_custom_call" | custom-call | tf_op jit(solution)/shard_map/pallas_call | solution.py:388

commit v6 on v5

--- a/solution.py
+++ b/solution.py
@@ -45,14 +45,18 @@
     cpart,
     ccore,
     cx,
-    cfirst,
-    csecond,
+    cfirst_y,
+    cfirst_z,
+    csecond_y,
+    csecond_z,
     cfull,
     gpart,
     gcore,
     gx,
-    gfirst,
-    gsecond,
+    gfirst_y,
+    gfirst_z,
+    gsecond_y,
+    gsecond_z,
     gpair,
     csum,
     gsum,
@@ -78,7 +82,7 @@
     hub_cols = local_cols // NX
     width = hub_cols // CHUNKS
     half = block // 2
-    quarter = half // 2
+    quarter = half // 4
 
     rows = lax.axis_index("rows")
     x = lax.axis_index("modes")
@@ -99,15 +103,23 @@
         return ((lax.rem(z + d, NZ) * NY + y) * 2 + core, x)
 
     sibling = ((z * NY + y) * 2 + (1 - core), x)
+    side = lax.rem(y, 2)
+    pair = lax.div(y, 2)
+    beside = y + 1 - 2 * side
+
+    def near(d, e, f=0):
+        row = beside if e else y
+        return ((z * NY + row) * 2 + (1 - core if f else core), x_peer(d))
+
+    group = [(d, e) for d in (2, 1, 3, 0) for e in (1, 0) if d or e]
 
     barrier = pltpu.get_barrier_semaphore()
-    for d in (4, 3, 5, 2, 6, 1, 7):
-        pl.semaphore_signal(barrier, inc=1, device_id=y_device(d), device_id_type=MESH)
-        pl.semaphore_signal(barrier, inc=1, device_id=z_device(d), device_id_type=MESH)
-    for d in (2, 1, 3):
-        pl.semaphore_signal(barrier, inc=1, device_id=x_device(d), device_id_type=MESH)
-    pl.semaphore_signal(barrier, inc=1, device_id=sibling, device_id_type=MESH)
-    pl.semaphore_wait(barrier, (NX - 1) + (NY - 1) + (NZ - 1) + 1)
+    y_devices = [y_device(d) for d in (4, 2, 6)]
+    z_devices = [z_device(d) for d in (4, 3, 5, 2, 6, 1, 7)]
+    partners = [near(d, e) for d, e in group] + y_devices + z_devices + [sibling, near(0, 1, 1)]
+    for partner in partners:
+        pl.semaphore_signal(barrier, inc=1, device_id=partner, device_id_type=MESH)
+    pl.semaphore_wait(barrier, len(partners))
 
     pending = []
 
@@ -157,6 +169,17 @@
     for k in range(WINDOW):
         fetch(k)
 
+    piece = hub_cols // PIECES
+    last = (PIECES - 1) * piece
+    extra_own = []
+    for d in range(1, NX):
+        there = pl.ds(pl.multiple_of(x_peer(d) * hub_cols + last, 128), piece)
+        pairs = ((phi_ref.at[:, there], phi_last.at[d - 1, block_rows(x)]), (s_ref.at[:, there], s_last.at[d - 1]))
+        for i, (src, dst) in enumerate(pairs):
+            copy = pltpu.make_async_copy(src, dst, last_own.at[i, d - 1])
+            copy.start()
+            extra_own.append(copy)
+
     acc = None
     for k in range(CHUNKS):
         for copy in own[k]:
@@ -170,52 +193,72 @@
         acc = term if acc is None else acc + term
     cpart[...] = acc.reshape(cpart.shape)
 
-    def reduce_grid(part, from_core, from_x, mid, first, second, total, ssem, rsem, meanwhile):
+    class Ring:
+        def __init__(self, slots, mine, devices, ssem, rsem):
+            for device in devices:
+                pltpu.make_async_remote_copy(
+                    src_ref=slots.at[mine],
+                    dst_ref=slots.at[mine],
+                    send_sem=ssem,
+                    recv_sem=rsem,
+                    device_id=device,
+                    device_id_type=MESH,
+                ).start()
+            self.all = pltpu.make_async_remote_copy(
+                src_ref=slots.at[pl.ds(0, len(devices))],
+                dst_ref=slots.at[pl.ds(0, len(devices))],
+                send_sem=ssem,
+                recv_sem=rsem,
+                device_id=devices[0],
+                device_id_type=MESH,
+            )
+            self.wait_recv = self.all.wait_recv
+            self.wait_send = self.all.wait_send
+
+    def ring(slots, mine, devices, ssem, rsem):
+        copies = Ring(slots, mine, devices, ssem, rsem)
+        pending.append(copies)
+        return copies
+
+    def reduce_grid(part, from_core, from_near, mid, first, second, total, ssem, rsem, meanwhile):
         copy = send(part.at[:, 1 - core], from_core, ssem.at[0], rsem.at[0], sibling)
         copy.wait_recv()
         mid[...] = part[:, core] + from_core[...]
         copies = []
-        for d in (2, 1, 3):
-            copies.append(send(mid.at[x_peer(d)], from_x.at[x], ssem.at[d], rsem.at[d], x_device(d)))
-        from_x[x] = mid[x]
+        for k, (d, e) in enumerate(group):
+            to_side = 1 - side if e else side
+            copies.append(
+                send(mid.at[x_peer(d), to_side], from_near.at[x, side], ssem.at[k + 1], rsem.at[k + 1], near(d, e))
+            )
+        from_near[x, side] = mid[x, side]
         meanwhile[0]()
         for copy in copies:
             copy.wait_recv()
+        value = jnp.sum(from_near[...].reshape((2 * NX,) + total.shape), axis=0)
+        along_y, along_z = first
+        along_y[pair] = value[:quarter]
+        along_z[z] = value[quarter:]
+        copies = [
+            ring(along_y, pair, y_devices, ssem.at[8], rsem.at[8]),
+            ring(along_z, z, z_devices, ssem.at[9], rsem.at[9]),
+        ]
         meanwhile[1]()
-        value = (from_x[0] + from_x[1]) + (from_x[2] + from_x[3])
-        first[0, y] = value[:quarter]
-        first[1, z] = value[quarter:]
-        base = NX
-        copies = []
-        for d in (4, 3, 5, 2, 6, 1, 7):
-            copies.append(
-                send(first.at[0, y], first.at[0, y], ssem.at[base + d], rsem.at[base + d], y_device(d))
-            )
-            copies.append(
-                send(first.at[1, z], first.at[1, z], ssem.at[base + 8 + d], rsem.at[base + 8 + d], z_device(d))
-            )
         meanwhile[2]()
         for copy in copies:
             copy.wait_recv()
-        second[0, z] = jnp.sum(first[0], axis=0)
-        second[1, y] = jnp.sum(first[1], axis=0)
-        base = NX + 16
-        copies = []
-        for d in (4, 3, 5, 2, 6, 1, 7):
-            copies.append(
-                send(second.at[0, z], second.at[0, z], ssem.at[base + d], rsem.at[base + d], z_device(d))
-            )
-            copies.append(
-                send(second.at[1, y], second.at[1, y], ssem.at[base + 8 + d], rsem.at[base + 8 + d], y_device(d))
-            )
+        then_z, then_y = second
+        then_z[z] = jnp.sum(along_y[...], axis=0)
+        then_y[pair] = jnp.sum(along_z[...], axis=0)
+        copies = [
+            ring(then_z, z, z_devices, ssem.at[10], rsem.at[10]),
+            ring(then_y, pair, y_devices, ssem.at[11], rsem.at[11]),
+        ]
         meanwhile[3]()
         for copy in copies:
             copy.wait_recv()
-        total[:quarter] = jnp.sum(second[0], axis=0)
-        total[quarter:] = jnp.sum(second[1], axis=0)
-
-    piece = hub_cols // PIECES
-    last = (PIECES - 1) * piece
+        total[:quarter] = jnp.sum(then_z[...], axis=0)
+        total[quarter:] = jnp.sum(then_y[...], axis=0)
+
     extra = []
 
     def nothing():
@@ -236,51 +279,34 @@
                     )
                 )
 
-    extra_own = []
-    for d in range(1, NX):
-        there = pl.ds(pl.multiple_of(x_peer(d) * hub_cols + last, 128), piece)
-        pairs = ((phi_ref.at[:, there], phi_last.at[d - 1, block_rows(x)]), (s_ref.at[:, there], s_last.at[d - 1]))
-        for i, (src, dst) in enumerate(pairs):
-            copy = pltpu.make_async_copy(src, dst, last_own.at[i, d - 1])
-            copy.start()
-            extra_own.append(copy)
-
     reduce_grid(
         cpart,
         ccore,
         cx,
         cmid,
-        cfirst,
-        csecond,
+        (cfirst_y, cfirst_z),
+        (csecond_z, csecond_y),
         csum,
         c_send,
         c_recv,
-        (nothing, gather_last, lambda: settle((NY - 1) + (NZ - 1) + (NX - 1) ** 2), nothing),
+        (nothing, gather_last, lambda: settle(2 + (NX - 1) ** 2), nothing),
     )
-    base = NX + 32
-    cfull[core, x] = csum[...]
+    cfull[core, x, side] = csum[...]
     copies = []
-    for d in (2, 1, 3):
-        copies.append((d, send(csum, cfull.at[core, x], c_send.at[base + d], c_recv.at[base + d], x_device(d))))
-    passed = [send(csum, cfull.at[core, x], c_send.at[base], c_recv.at[base], sibling)]
-    for d, copy in copies[1:] + copies[:1]:
+    for k, (d, e) in enumerate(group):
+        copies.append(
+            send(csum, cfull.at[core, x, side], c_send.at[12 + k], c_recv.at[12 + k], near(d, e))
+        )
+    for copy in copies:
         copy.wait_recv()
-        origin = lax.rem(x + NX - d, NX)
-        passed.append(
-            send(
-                cfull.at[core, origin],
-                cfull.at[core, origin],
-                c_send.at[base + NX + d],
-                c_recv.at[base + NX + d],
-                sibling,
-            )
-        )
-    for copy in passed:
-        copy.wait_recv()
-    coef_ref[:half] = cfull[0, x]
-    coef_ref[half:] = cfull[1, x]
+    copy = send(cfull.at[core], cfull.at[core], c_send.at[20], c_recv.at[20], sibling)
+    copy.wait_recv()
+
+    def rows_of(a):
+        return [cfull[c, a].reshape(half, NX * block) for c in range(2)]
+
     coefficients = jnp.concatenate(
-        [cfull[c, a] for a in range(NX) for c in range(2)], axis=0
+        [part for a in range(NX) for part in rows_of(a)], axis=0
     )
 
     returns, own = [], []
@@ -334,30 +360,38 @@
             copy.wait()
         for copy in extra:
             copy.wait_recv()
-        mine = jnp.concatenate([cfull[0, x], cfull[1, x]], axis=0)
+        mine = jnp.concatenate(rows_of(x), axis=0)
+        coef_ref[...] = mine
         for d in range(1, NX):
             there = pl.ds(pl.multiple_of(x_peer(d) * hub_cols + last, 128), piece)
             res_ref[:, there] = s_last[d - 1] - product(mine, phi_last[d - 1], 0)
 
-    later = (NX - 1) * (PIECES - 1) + (NY - 1) + (NZ - 1)
+    later = (NX - 1) * (PIECES - 1) + 2
 
     reduce_grid(
         gpart,
         gcore,
         gx,
         gmid,
-        gfirst,
-        gsecond,
+        (gfirst_y, gfirst_z),
+        (gsecond_z, gsecond_y),
         gsum,
         g_send,
         g_recv,
-        (send_some, send_the_rest, own_residual, lambda: settle(later + (NY - 1) + (NZ - 1))),
+        (send_some, send_the_rest, own_residual, lambda: settle(later + 2)),
     )
-    base = NX + 32
-    gpair[core] = gsum[...]
-    copy = send(gpair.at[core], gpair.at[core], g_send.at[base], g_recv.at[base], sibling)
-    copy.wait_recv()
-    gram = jnp.concatenate([gpair[0], gpair[1]], axis=0) / total_rows
+    gpair[core, side] = gsum[...]
+    copies = []
+    for k, partner in enumerate((near(0, 1, 1), near(0, 1), sibling)):
+        copies.append(send(gpair.at[core, side], gpair.at[core, side], g_send.at[12 + k], g_recv.at[12 + k], partner))
+    for done in returns:
+        done.wait_recv()
+    for done in own:
+        done.wait()
+    settle(3)
+    for copy in copies:
+        copy.wait_recv()
+    gram = gpair[...].reshape(block, NX * block) / total_rows
     gram_ref[...] = gram
     column = lax.broadcasted_iota(jnp.int32, gram.shape, 1)
     row = lax.broadcasted_iota(jnp.int32, gram.shape, 0)
@@ -365,10 +399,6 @@
     diagonal = functools.reduce(jnp.add, [diagonal[:, a * block : (a + 1) * block] for a in range(NX)])
     norm_ref[...] = jnp.sqrt(diagonal)
 
-    for copy in returns:
-        copy.wait_recv()
-    for copy in own:
-        copy.wait()
     settle(0)
 
 
@@ -399,15 +429,16 @@
     block, local_cols = modes_basis.shape
     size = block * NX
     hub_cols = local_cols // NX
-    half, quarter = block // 2, block // 4
+    share = block // 4
     total_rows = local_cols * lax.axis_size("rows")
     f32 = jnp.float32
-    sems = NX + 32 + 2 * NX
+    sems = 24
     hbm = pl.BlockSpec(memory_space=pltpu.HBM)
     vmem = pl.BlockSpec(memory_space=pltpu.VMEM)
-    part = pltpu.VMEM((NX, 2, half, size), f32)
-    quad = pltpu.VMEM((NX, half, size), f32)
-    ring = pltpu.VMEM((2, NY, quarter, size), f32)
+    part = pltpu.VMEM((NX, 2, 2, share, size), f32)
+    near = pltpu.VMEM((NX, 2, share, size), f32)
+    rings = [pltpu.VMEM((n, share // 2, size), f32) for n in (NY // 2, NZ, NY // 2, NZ)]
+    own = pltpu.VMEM((share, size), f32)
     outs = pl.pallas_call(
         functools.partial(kernel, float(total_rows)),
         out_shape=(
@@ -423,21 +454,19 @@
             pltpu.VMEM((size, hub_cols), f32),
             pltpu.VMEM((size, hub_cols), f32),
             part,
-            quad,
-            quad,
-            ring,
-            ring,
-            pltpu.VMEM((2, NX, half, size), f32),
+            near,
+            near,
+            *rings,
+            pltpu.VMEM((2, NX, 2, share, size), f32),
             part,
-            quad,
-            quad,
-            ring,
-            ring,
-            pltpu.VMEM((2, half, size), f32),
-            pltpu.VMEM((half, size), f32),
-            pltpu.VMEM((half, size), f32),
-            quad,
-            quad,
+            near,
+            near,
+            *rings,
+            pltpu.VMEM((2, 2, share, size), f32),
+            own,
+            own,
+            near,
+            near,
             pltpu.SemaphoreType.DMA((CHUNKS, 2, NX - 1)),
             pltpu.SemaphoreType.DMA((CHUNKS, 2, NX - 1)),
             pltpu.SemaphoreType.DMA((CHUNKS, 2)),

time: 96.7 us -> 96.3 us (level)
  no operation moved by 1% of the time
where the time goes in v6:
time: 96.3 us; the launch traced here: 96.1 us
  Pallas kernels  95.5 us (99%)
    pallas_call x1, Pallas kernels, per_device(): pl.pallas_call(functools.partial(kernel, float(total_rows)), out_shape=(p...  94.3 us

profile of v6, /device:TPU:1, one launch (start us, length us, event | category | flops | bytes accessed | tf_op | source)
XLA Modules:
  0.0 96.1 jit_solution(11826885479047134782)
XLA Ops:
  0.6 94.3 %shard_map.57 = (f32[64,256]{1,0:T(8,128)S(1)}, f32[64,6144]{1,0:T(8,128)S(1)}, f32[64,256]{1,0:T(8,128)S(1)}, f32[1,64]{1,0:T(1,128)S(1)}) custom-call(f32[64,6144]{1,0:T(8,128)} %phi_ref.1, f32[64,6144]{1,0:T(8,128)} %s_ref.1), custom_call_target="tpu_custom_call" | custom-call | flops 603979776 | bytes 4718592 | tf_op jit(solution)/shard_map/pallas_call | solution.py:442
  94.9 1.2 %shard_map.58 = (f32[64,256]{1,0:T(8,128)}, f32[64,6144]{1,0:T(8,128)}, f32[64,256]{1,0:T(8,128)}, f32[1,64]{1,0:T(1,128)}) custom-call(f32[64,256]{1,0:T(8,128)S(1)} %get-tuple-element.12.refs_0_, f32[64,6144]{1,0:T(8,128)S(1)} %get-tuple-element.13.refs_1_, f32[64,256]{1,0:T(8,128)S(1)} %get-tuple-element.14.refs_2_, f32[1,64]{1,0:T(1,128)S(1)} %get-tuple-element.15.refs_3_), custom_call_target="tpu_custom_call" | custom-call | tf_op jit(solution)/shard_map/pallas_call | solution.py:418

commit v7 on v6

--- a/solution.py
+++ b/solution.py
@@ -297,10 +297,17 @@
         copies.append(
             send(csum, cfull.at[core, x, side], c_send.at[12 + k], c_recv.at[12 + k], near(d, e))
         )
-    for copy in copies:
+    passed = []
+    for d in (0, 1, 3, 2):
+        for (distance, _), copy in zip(group, copies):
+            if distance == d:
+                copy.wait_recv()
+        origin = lax.rem(x + NX - d, NX)
+        passed.append(
+            send(cfull.at[core, origin], cfull.at[core, origin], c_send.at[20 + d], c_recv.at[20 + d], sibling)
+        )
+    for copy in passed:
         copy.wait_recv()
-    copy = send(cfull.at[core], cfull.at[core], c_send.at[20], c_recv.at[20], sibling)
-    copy.wait_recv()
 
     def rows_of(a):
         return [cfull[c, a].reshape(half, NX * block) for c in range(2)]

time: 96.3 us -> 96.2 us (level)
  no operation moved by 1% of the time
where the time goes in v7:
time: 96.2 us; the launch traced here: 96.1 us
  Pallas kernels  95.4 us (99%)
    pallas_call x1, Pallas kernels, per_device(): pl.pallas_call(functools.partial(kernel, float(total_rows)), out_shape=(p...  94.2 us

profile of v7, /device:TPU:1, one launch (start us, length us, event | category | flops | bytes accessed | tf_op | source)
XLA Modules:
  0.0 96.1 jit_solution(15333768272650308223)
XLA Ops:
  0.6 94.2 %shard_map.57 = (f32[64,256]{1,0:T(8,128)S(1)}, f32[64,6144]{1,0:T(8,128)S(1)}, f32[64,256]{1,0:T(8,128)S(1)}, f32[1,64]{1,0:T(1,128)S(1)}) custom-call(f32[64,6144]{1,0:T(8,128)} %phi_ref.1, f32[64,6144]{1,0:T(8,128)} %s_ref.1), custom_call_target="tpu_custom_call" | custom-call | flops 603979776 | bytes 4718592 | tf_op jit(solution)/shard_map/pallas_call | solution.py:449
  94.8 1.2 %shard_map.58 = (f32[64,256]{1,0:T(8,128)}, f32[64,6144]{1,0:T(8,128)}, f32[64,256]{1,0:T(8,128)}, f32[1,64]{1,0:T(1,128)}) custom-call(f32[64,256]{1,0:T(8,128)S(1)} %get-tuple-element.12.refs_0_, f32[64,6144]{1,0:T(8,128)S(1)} %get-tuple-element.13.refs_1_, f32[64,256]{1,0:T(8,128)S(1)} %get-tuple-element.14.refs_2_, f32[1,64]{1,0:T(1,128)S(1)} %get-tuple-element.15.refs_3_), custom_call_target="tpu_custom_call" | custom-call | tf_op jit(solution)/shard_map/pallas_call | solution.py:425
